TPU v7x, 512 devices: a whole 4x4x16 slice. The times are simulated.
512 devices in a mesh: sec: 2 (over x_lo), lat: 8 (over y, core), lon: 32 (over z, x_hi).
Axes of the slice: x: 4 (x_hi: 2, x_lo: 2; x = x_hi * 2 + x_lo), y: 4, z: 16, core: 2. Of those that a mesh axis runs over, the one named last changes fastest.
Arguments:
- state: bfloat16 [2, 512, 1440, 256], P('sec', 'lat', 'lon'), may hold values from -6 to 6
- wet_mask: int32 [512, 1440], P('lat', 'lon'), may hold values 0 or 1
- tap_offsets: int32 [512, 3, 3], P('lat'), may hold values from -16 to 16
- conv_weight: bfloat16 [2, 9, 256, 256], P('sec'), may hold values from -0.125 to 0.125
- couple_proj: bfloat16 [2, 256, 128], replicated, may hold values from -0.375 to 0.375
- couple_in: bfloat16 [2, 128, 256], P('sec'), may hold values from -0.5 to 0.5
- norm_gain: float32 [2, 256], P('sec'), may hold values from 0.5 to 1.5
- up_weight: bfloat16 [2, 256, 512], P('sec'), may hold values from -0.375 to 0.375
- down_weight: bfloat16 [2, 512, 256], P('sec'), may hold values from -0.25 to 0.25
Outputs:
- new_state: bfloat16 [2, 512, 1440, 256], P('sec', 'lat', 'lon')
All inputs are finite; a program needn't handle non-finite values. No bound on the sum of `wet_mask` on one device may be relied on, other than what follows from the above.
Results may differ from a plain program's by a relative error of at most 0.0038.
Values may be sent and summed in bfloat16 or wider, within the bound.
A program may use at most 128 MiB of HBM per device.

v0:
```python
import jax
import jax.numpy as jnp
from jax import lax
from jax.sharding import PartitionSpec as P

HALO = 16


def partner(block, axis, stride):
    count = lax.axis_size(axis)
    route = []
    for low in range(count):
        high = low | 1 << stride
        if high != low and high < count:
            route += [(low, high), (high, low)]
    return lax.ppermute(block, axis, route)


def extended_2(shard, sides, width, wrap):
    for axis, dim in sides:
        count, length = (lax.axis_size(axis), shard.shape[dim])
        up = [(i, (i + 1) % count) for i in range(count if wrap else count - 1)]
        down = [(j, i) for i, j in up]
        last = lax.slice_in_dim(shard, length - width, length, axis=dim)
        initial = lax.slice_in_dim(shard, 0, width, axis=dim)
        before = lax.ppermute(last, axis, up)
        after = lax.ppermute(initial, axis, down)
        shard = jnp.concatenate([before, shard, after], axis=dim)
    return shard


def local(
    state,
    wet_mask,
    tap_offsets,
    conv_weight,
    couple_proj,
    couple_in,
    norm_gain,
    up_weight,
    down_weight,
):
    field = state[0]
    section = lax.axis_index("sec")
    wet = wet_mask.astype(jnp.float32)
    ones = jnp.ones_like(wet)
    keep = jnp.where(section == 0, ones, wet)
    other_field = partner(field, "sec", 0)
    other_keep = jnp.where(section == 0, wet, ones)
    other_proj = lax.dynamic_index_in_dim(couple_proj, 1 - section, 0, keepdims=False)
    projected = jnp.einsum(
        "ijc,ck->ijk", other_field, other_proj, preferred_element_type=jnp.float32
    )
    received = (jax.nn.silu(projected) * other_keep[:, :, None]).astype(jnp.bfloat16)
    row_ext = extended_2(field, (("lat", 0),), 1, False)
    extended = extended_2(row_ext, (("lon", 1),), HALO, True)
    lat_rows = field.shape[0]
    lon_cols = field.shape[1]
    channels = field.shape[2]
    ext_cols = extended.shape[1]
    filters = conv_weight[0]
    columns = jnp.arange(lon_cols, dtype=jnp.int32)
    positions = jnp.arange(ext_cols, dtype=jnp.int32)
    acc = jnp.zeros((lat_rows, lon_cols, channels), jnp.float32)
    for shift_row in range(3):
        band = extended[shift_row : shift_row + lat_rows]
        for tap in range(3):
            target = columns[None, :] + HALO + tap_offsets[:, shift_row, tap][:, None]
            select = (positions[None, None, :] == target[:, :, None]).astype(jnp.bfloat16)
            picked = jnp.einsum(
                "ijm,imc->ijc", select, band, preferred_element_type=jnp.float32
            ).astype(jnp.bfloat16)
            acc = acc + jnp.einsum(
                "ijc,cd->ijd",
                picked,
                filters[3 * shift_row + tap],
                preferred_element_type=jnp.float32,
            )
    pre = acc + jnp.einsum(
        "ijk,kc->ijc", received, couple_in[0], preferred_element_type=jnp.float32
    )
    meansq = jnp.mean(pre * pre, axis=-1, keepdims=True)
    normed = (pre / jnp.sqrt(meansq + 1e-05) * norm_gain[0]).astype(jnp.bfloat16)
    hidden = jax.nn.gelu(
        jnp.einsum("ijc,ch->ijh", normed, up_weight[0], preferred_element_type=jnp.float32)
    ).astype(jnp.bfloat16)
    update = jnp.einsum("ijh,hc->ijc", hidden, down_weight[0], preferred_element_type=jnp.float32)
    result = (field.astype(jnp.float32) + keep[:, :, None] * update).astype(jnp.bfloat16)
    return result[None]


def solution(mesh):
    in_specs = (
        P("sec", "lat", "lon", None),
        P("lat", "lon"),
        P("lat", None, None),
        P("sec", None, None, None),
        P(),
        P("sec", None, None),
        P("sec", None),
        P("sec", None, None),
        P("sec", None, None),
    )
    out_specs = P("sec", "lat", "lon", None)
    return jax.shard_map(local, mesh=mesh, in_specs=in_specs, out_specs=out_specs, check_vma=False)
```

profile of v0, /device:TPU:7, one launch (start us, length us, event | category | flops | bytes accessed | tf_op | source)
XLA Modules:
  0.0 122.4 jit_solution(595223517340505497)
XLA Ops:
  0.0 2.2 %copy.78 = bf16[1,64,45,256]{3,2,1,0:T(8,128)(2,1)S(1)} copy(bf16[1,64,45,256]{3,1,2,0:T(8,128)(2,1)} %param.9) | data formatting | bytes 2949120 | tf_op args[0]
  2.3 3.8 %collective-permute-start = (bf16[1,45,256]{2,1,0:T(8,128)(2,1)S(1)}, bf16[1,45,256]{2,1,0:T(8,128)(2,1)S(1)}, u32[]{:S(2)}, u32[]{:S(2)}) collective-permute-start(bf16[1,45,256]{2,1,0:T(8,128)(2,1)S(1)} %get-tuple-element.7), channel_id=1, source_target_pairs={{0,32},{32,64},{64,96},{96,128},{128,160},{160,192},{192,224},{1,3... | collective-permute-start | bytes 69128 | tf_op jit(solution)/shard_map/ppermute | solution.py:26
  6.0 1.9 %collective-permute-start.1 = (bf16[1,45,256]{2,1,0:T(8,128)(2,1)S(1)}, bf16[1,45,256]{2,1,0:T(8,128)(2,1)S(1)}, u32[]{:S(2)}, u32[]{:S(2)}) collective-permute-start(bf16[1,45,256]{2,1,0:T(8,128)(2,1)S(1)} %get-tuple-element.8), channel_id=1, source_target_pairs={{32,0},{64,32},{96,64},{128,96},{160,128},{192,160},{224,192},{33,... | collective-permute-start | bytes 69128 | tf_op jit(solution)/shard_map/ppermute | solution.py:27
  8.0 2.5 %collective-permute-start.4 = (bf16[64,45,256]{2,0,1:T(8,128)(2,1)}, bf16[64,45,256]{2,0,1:T(8,128)(2,1)}, u32[]{:S(2)}, u32[]{:S(2)}) collective-permute-start(bf16[64,45,256]{2,0,1:T(8,128)(2,1)} %bitcast.32), channel_id=1, source_target_pairs={{0,256},{256,0},{1,257},{257,1},{2,258},{258,2},{3,259},{259,3},{4... | collective-permute-start | bytes 4423688 | tf_op jit(solution)/shard_map/ppermute | solution.py:16
  10.6 1.0 collective-permute-done.1
  11.8 4.4 %collective-permute-start.2 = (bf16[66,16,256]{2,1,0:T(8,128)(2,1)S(1)}, bf16[66,16,256]{2,1,0:T(8,128)(2,1)S(1)}, u32[]{:S(2)}, u32[]{:S(2)}) collective-permute-start(bf16[66,16,256]{2,1,0:T(8,128)(2,1)S(1)} %get-tuple-element.5), channel_id=1, source_target_pairs={{0,1},{1,2},{2,3},{3,4},{4,5},{5,6},{6,7},{7,8},{8,9},{9,10},{10,1... | collective-permute-start | bytes 1622024 | tf_op jit(solution)/shard_map/ppermute | solution.py:26
  16.2 2.8 %collective-permute-start.3 = (bf16[66,16,256]{2,1,0:T(8,128)(2,1)S(1)}, bf16[66,16,256]{2,1,0:T(8,128)(2,1)S(1)}, u32[]{:S(2)}, u32[]{:S(2)}) collective-permute-start(bf16[66,16,256]{2,1,0:T(8,128)(2,1)S(1)} %get-tuple-element.6), channel_id=1, source_target_pairs={{1,0},{2,1},{3,2},{4,3},{5,4},{6,5},{7,6},{8,7},{9,8},{10,9},{11,1... | collective-permute-start | bytes 1622024 | tf_op jit(solution)/shard_map/ppermute | solution.py:27
  19.3 51.5 %collective-permute-done.2 = bf16[66,16,256]{2,1,0:T(8,128)(2,1)S(1)} collective-permute-done((bf16[66,16,256]{2,1,0:T(8,128)(2,1)S(1)}, bf16[66,16,256]{2,1,0:T(8,128)(2,1)S(1)}, u32[]{:S(2)}, u32[]{:S(2)}) %collective-permute-start.2) | collective-permute-done | bytes 540704 | tf_op jit(solution)/shard_map/ppermute | solution.py:26
  71.4 0.9 fusion.51
  74.2 2.2 %fusion.68 = f32[64,45,256]{2,0,1:T(8,128)} fusion(bf16[64,45,256]{2,1,0:T(8,128)(2,1)S(1)} %fusion.48, bf16[1,9,256,256]{3,2,1,0:T(8,128)(2,1)S(1)} %copy-done.1), kind=kOutput, calls=%fused_computation.63 | convolution fusion | flops 377487360 | bytes 4653056 | tf_op jit(solution)/shard_map/ijc,cd->ijd/dot_general | solution.py:73
  77.3 2.3 %fusion.70 = f32[64,45,256]{2,0,1:T(8,128)} fusion(bf16[64,45,256]{2,1,0:T(8,128)(2,1)S(1)} %fusion.45, bf16[1,9,256,256]{3,2,1,0:T(8,128)(2,1)S(1)} %copy-done.1), kind=kOutput, calls=%fused_computation.65 | convolution fusion | flops 377487360 | bytes 4653056 | tf_op jit(solution)/shard_map/ijc,cd->ijd/dot_general | solution.py:73
  80.5 2.3 %fusion.72 = f32[64,45,256]{2,0,1:T(8,128)} fusion(bf16[64,45,256]{2,1,0:T(8,128)(2,1)S(1)} %fusion.42, bf16[1,9,256,256]{3,2,1,0:T(8,128)(2,1)S(1)} %copy-done.1), kind=kOutput, calls=%fused_computation.67 | convolution fusion | flops 377487360 | bytes 4653056 | tf_op jit(solution)/shard_map/ijc,cd->ijd/dot_general | solution.py:73
  83.6 2.2 %fusion.74 = f32[64,45,256]{2,0,1:T(8,128)} fusion(bf16[64,45,256]{2,1,0:T(8,128)(2,1)S(1)} %fusion.39, bf16[1,9,256,256]{3,2,1,0:T(8,128)(2,1)S(1)} %copy-done.1), kind=kOutput, calls=%fused_computation.69 | convolution fusion | flops 377487360 | bytes 4653056 | tf_op jit(solution)/shard_map/ijc,cd->ijd/dot_general | solution.py:73
  86.7 0.9 fusion.33
  87.6 0.9 fusion.30
  88.5 1.1 fusion.54
  89.6 2.3 %fusion.76 = f32[64,45,256]{2,0,1:T(8,128)} fusion(bf16[64,45,256]{2,1,0:T(8,128)(2,1)S(1)} %fusion.36, bf16[1,9,256,256]{3,2,1,0:T(8,128)(2,1)S(1)} %copy-done.1), kind=kOutput, calls=%fused_computation.71 | convolution fusion | flops 377487360 | bytes 4653056 | tf_op jit(solution)/shard_map/ijc,cd->ijd/dot_general | solution.py:73
  91.9 2.2 %fusion.78 = f32[64,45,256]{2,0,1:T(8,128)} fusion(bf16[64,45,256]{2,1,0:T(8,128)(2,1)S(1)} %fusion.33, bf16[1,9,256,256]{3,2,1,0:T(8,128)(2,1)S(1)} %copy-done.1), kind=kOutput, calls=%fused_computation.73 | convolution fusion | flops 377487360 | bytes 4653056 | tf_op jit(solution)/shard_map/ijc,cd->ijd/dot_general | solution.py:73
  94.1 2.2 %fusion.80 = f32[64,45,256]{2,0,1:T(8,128)} fusion(bf16[64,45,256]{2,1,0:T(8,128)(2,1)S(1)} %fusion.30, bf16[1,9,256,256]{3,2,1,0:T(8,128)(2,1)S(1)} %copy-done.1), kind=kOutput, calls=%fused_computation.75 | convolution fusion | flops 377487360 | bytes 4653056 | tf_op jit(solution)/shard_map/ijc,cd->ijd/dot_general | solution.py:73
  96.3 2.3 %fusion.64 = f32[64,45,256]{2,0,1:T(8,128)} fusion(bf16[64,45,256]{2,1,0:T(8,128)(2,1)S(1)} %fusion.54, bf16[1,9,256,256]{3,2,1,0:T(8,128)(2,1)S(1)} %copy-done.1), kind=kOutput, calls=%fused_computation.59 | convolution fusion | flops 377487360 | bytes 4653056 | tf_op jit(solution)/shard_map/ijc,cd->ijd/dot_general | solution.py:73
  98.6 11.5 %multiply_reduce_fusion = (f32[64,45]{0,1:T(8,128)S(1)}, f32[64,45,256]{2,0,1:T(8,128)}) fusion(bf16[1,128,256]{2,1,0:T(8,128)(2,1)S(1)} %copy-done.2, bf16[64,45,256]{2,0,1:T(8,128)(2,1)} %collective-permute-done.4, f32[64,45]{0,1:T(8,128)S(1)} %get-tuple-element.12, bf16[2,256,128]{2,1,0:T(8,128)(2,1)S(1)} %copy-done.3, s32[]{:T(128)S(6)} %select_n.18, ...), kind=kOutput, calls=%fused_computation.13 | convolution fusion | flops 387806400 | bytes 31132932 | tf_op jit(solution)/shard_map/ijk,kc->ijc/dot_general | solution.py:79
  110.2 4.1 %fusion.7 = bf16[64,45,512]{2,0,1:T(8,128)(2,1)S(1)} fusion(f32[64,45,256]{2,0,1:T(8,128)} %get-tuple-element.32, f32[256]{0:T(256)S(1)} %bitcast.118, f32[64,45]{0,1:T(8,128)S(1)} %add_sqrt_fusion, bf16[1,256,512]{2,1,0:T(8,128)(2,1)S(1)} %copy-done), kind=kOutput, calls=%fused_computation.8 | convolution fusion | flops 770457600 | bytes 6172928 | tf_op jit(solution)/shard_map/ijc,ch->ijh/dot_general | solution.py:85
  114.4 6.4 %fusion.57 = bf16[1,64,45,256]{3,2,1,0:T(8,128)(2,1)S(1)} fusion(bf16[64,45,512]{2,0,1:T(8,128)(2,1)S(1)} %fusion.7, f32[64,45]{1,0:T(8,128)S(1)} %copy.33, bf16[1,512,256]{2,1,0:T(8,128)(2,1)S(1)} %copy-done.6, bf16[1,64,45,256]{3,1,2,0:T(8,128)(2,1)} %param.9), kind=kOutput, calls=%fused_computation.52 | convolution fusion | flops 757923840 | bytes 6171904 | tf_op jit(solution)/shard_map/ijh,hc->ijc/dot_general | solution.py:87
  120.8 1.6 %copy.47 = bf16[1,64,45,256]{3,1,2,0:T(8,128)(2,1)} copy(bf16[1,64,45,256]{3,2,1,0:T(8,128)(2,1)S(1)} %fusion.57) | data formatting | bytes 2949120 | tf_op jit(solution)/shard_map/broadcast_in_dim | solution.py:89
  (34 shorter events, 6.6 us)
Async XLA Ops:
  0.0 110.2 %copy-start = (bf16[1,256,512]{2,1,0:T(8,128)(2,1)S(1)}, bf16[1,256,512]{2,1,0:T(8,128)(2,1)}, u32[]{:S(2)}) copy-start(bf16[1,256,512]{2,1,0:T(8,128)(2,1)} %param.16) | copy-start | bytes 786436
  0.0 10.4 %copy-start.4 = (s32[64,45]{0,1:T(8,128)S(1)}, s32[64,45]{0,1:T(8,128)}, u32[]{:S(2)}) copy-start(s32[64,45]{0,1:T(8,128)} %param.10) | copy-start | bytes 34564
  0.0 19.1 %copy-start.5 = (s32[64,3,3]{0,2,1:T(4,128)S(1)}, s32[64,3,3]{0,2,1:T(4,128)}, u32[]{:S(2)}) copy-start(s32[64,3,3]{0,2,1:T(4,128)} %param.11) | copy-start | bytes 6916
  2.3 8.3 %collective-permute-start = (bf16[1,45,256]{2,1,0:T(8,128)(2,1)S(1)}, bf16[1,45,256]{2,1,0:T(8,128)(2,1)S(1)}, u32[]{:S(2)}, u32[]{:S(2)}) collective-permute-start(bf16[1,45,256]{2,1,0:T(8,128)(2,1)S(1)} %get-tuple-element.7), channel_id=1, source_target_pairs={{0,32},{32,64},{64,96},{96,128},{128,160},{160,192},{192,224},{1,3... | collective-permute-start | bytes 69128 | tf_op jit(solution)/shard_map/ppermute | solution.py:26
  6.0 5.5 %collective-permute-start.1 = (bf16[1,45,256]{2,1,0:T(8,128)(2,1)S(1)}, bf16[1,45,256]{2,1,0:T(8,128)(2,1)S(1)}, u32[]{:S(2)}, u32[]{:S(2)}) collective-permute-start(bf16[1,45,256]{2,1,0:T(8,128)(2,1)S(1)} %get-tuple-element.8), channel_id=1, source_target_pairs={{32,0},{64,32},{96,64},{128,96},{160,128},{192,160},{224,192},{33,... | collective-permute-start | bytes 69128 | tf_op jit(solution)/shard_map/ppermute | solution.py:27
  8.0 90.6 %collective-permute-start.4 = (bf16[64,45,256]{2,0,1:T(8,128)(2,1)}, bf16[64,45,256]{2,0,1:T(8,128)(2,1)}, u32[]{:S(2)}, u32[]{:S(2)}) collective-permute-start(bf16[64,45,256]{2,0,1:T(8,128)(2,1)} %bitcast.32), channel_id=1, source_target_pairs={{0,256},{256,0},{1,257},{257,1},{2,258},{258,2},{3,259},{259,3},{4... | collective-permute-start | bytes 4423688 | tf_op jit(solution)/shard_map/ppermute | solution.py:16
  11.8 58.9 %collective-permute-start.2 = (bf16[66,16,256]{2,1,0:T(8,128)(2,1)S(1)}, bf16[66,16,256]{2,1,0:T(8,128)(2,1)S(1)}, u32[]{:S(2)}, u32[]{:S(2)}) collective-permute-start(bf16[66,16,256]{2,1,0:T(8,128)(2,1)S(1)} %get-tuple-element.5), channel_id=1, source_target_pairs={{0,1},{1,2},{2,3},{3,4},{4,5},{5,6},{6,7},{7,8},{8,9},{9,10},{10,1... | collective-permute-start | bytes 1622024 | tf_op jit(solution)/shard_map/ppermute | solution.py:26
  16.2 54.5 %collective-permute-start.3 = (bf16[66,16,256]{2,1,0:T(8,128)(2,1)S(1)}, bf16[66,16,256]{2,1,0:T(8,128)(2,1)S(1)}, u32[]{:S(2)}, u32[]{:S(2)}) collective-permute-start(bf16[66,16,256]{2,1,0:T(8,128)(2,1)S(1)} %get-tuple-element.6), channel_id=1, source_target_pairs={{1,0},{2,1},{3,2},{4,3},{5,4},{6,5},{7,6},{8,7},{9,8},{10,9},{11,1... | collective-permute-start | bytes 1622024 | tf_op jit(solution)/shard_map/ppermute | solution.py:27
  72.3 1.3 %copy-start.1 = (bf16[1,9,256,256]{3,2,1,0:T(8,128)(2,1)S(1)}, bf16[1,9,256,256]{3,2,1,0:T(8,128)(2,1)}, u32[]{:S(2)}) copy-start(bf16[1,9,256,256]{3,2,1,0:T(8,128)(2,1)} %param.12) | copy-start | bytes 3538948
  96.3 2.3 %copy-start.2 = (bf16[1,128,256]{2,1,0:T(8,128)(2,1)S(1)}, bf16[1,128,256]{2,1,0:T(8,128)(2,1)}, u32[]{:S(2)}) copy-start(bf16[1,128,256]{2,1,0:T(8,128)(2,1)} %param.14) | copy-start | bytes 196612
  96.3 2.3 %copy-start.3 = (bf16[2,256,128]{2,1,0:T(8,128)(2,1)S(1)}, bf16[2,256,128]{2,1,0:T(8,128)(2,1)}, u32[]{:S(2)}) copy-start(bf16[2,256,128]{2,1,0:T(8,128)(2,1)} %param.13) | copy-start | bytes 393220
  98.6 11.6 %copy-start.7 = (f32[1,256]{1,0:T(1,128)S(1)}, f32[1,256]{1,0:T(1,128)}, u32[]{:S(2)}) copy-start(f32[1,256]{1,0:T(1,128)} %param.15) | copy-start | bytes 3076
  110.2 4.2 %copy-start.6 = (bf16[1,512,256]{2,1,0:T(8,128)(2,1)S(1)}, bf16[1,512,256]{2,1,0:T(8,128)(2,1)}, u32[]{:S(2)}) copy-start(bf16[1,512,256]{2,1,0:T(8,128)(2,1)} %param.17) | copy-start | bytes 786436
where the time goes:
time: 123 us; the launch traced here: 122 us
  waiting for transfers between devices  52.5 us (43%)
  matrix products  48.8 us (40%)
  starting transfers between devices  15.4 us (13%)
  local copies, waits for them, and re-layouts  4.4 us (4%)
    ppermute x2, waiting for transfers between devices, extended_2(): before = lax.ppermute(last, axis, up)  51.5 us
    dot_general x9, matrix products, local(): jnp.einsum('ijc,cd->ijd', picked, filters[3 * shift_row + tap], preferred...  18.7 us
    dot_general x1, matrix products, local(): jnp.einsum('ijk,kc->ijc', received, couple_in[0], preferred_element_type=...  11.5 us
    ppermute x2, starting transfers between devices, extended_2(): before = lax.ppermute(last, axis, up)  8.15 us
    dot_general x9, matrix products, local(): jnp.einsum('ijm,imc->ijc', select, band, preferred_element_type=jnp.float32)  8.01 us
    dot_general x1, matrix products, local(): jnp.einsum('ijh,hc->ijc', hidden, down_weight[0], preferred_element_type=...  6.42 us
    ppermute x2, starting transfers between devices, extended_2(): after = lax.ppermute(initial, axis, down)  4.74 us
    dot_general x1, matrix products, local(): jnp.einsum('ijc,ch->ijh', normed, up_weight[0], preferred_element_type=jn...  4.15 us
  transfers between devices with their start and end apart: 5, of which 2 were waited for; matrix products, arithmetic and copies ran while one was open for 23% of the time, Pallas kernels for 0%

commit v1 on v0

v1 whole, which is shorter than its diff:
```python
import functools
import math

import jax
import jax.numpy as jnp
from jax import lax
from jax.experimental import pallas as pl
from jax.experimental.pallas import tpu as pltpu
from jax.sharding import PartitionSpec as P

HALO = 16
ROWS = 64
COLS = 45
SLOTS = 48
EXT = SLOTS + 2 * HALO
C = 256
K = 128
HID = 512
STEP = 8
STEPS = ROWS // STEP
TAPS = 9
MESH = pl.DeviceIdType.MESH


def kernel(
    x_ref,
    wet_ref,
    off_ref,
    cw_ref,
    cp_ref,
    ci_ref,
    gain_ref,
    up_ref,
    down_ref,
    out_ref,
    ext,
    raw_l,
    raw_r,
    mid_out,
    mid_in,
    diff,
    wet_q,
    picks,
    load_sem,
    s1_send,
    s1_recv,
    s2_send,
    s2_recv,
    f_send,
    f_recv,
    lat_send,
    lat_recv,
):
    sec = lax.axis_index("sec")
    la = lax.axis_index("lat")
    lo = lax.axis_index("lon")
    n_lat = lax.axis_size("lat")
    n_lon = lax.axis_size("lon")
    other = 1 - sec
    west, east = lax.rem(lo + n_lon - 1, n_lon), lax.rem(lo + 1, n_lon)
    north, south = lax.rem(la + n_lat - 1, n_lat), lax.rem(la + 1, n_lat)
    partner = (other, la, lo)
    to_west = (other, la, west)
    to_east = (other, la, east)
    to_north = (sec, north, lo)
    to_south = (sec, south, lo)

    load = pltpu.make_async_copy(x_ref, ext.at[pl.ds(1, ROWS), pl.ds(HALO, SLOTS)], load_sem)
    load.start()

    barrier = pltpu.get_barrier_semaphore()
    for peer in (partner, to_west, to_east, to_north, to_south):
        pl.semaphore_signal(barrier, inc=1, device_id=peer, device_id_type=MESH)

    def rows_of(c):
        if isinstance(c, int) and c < 2:
            return pl.ds(1 if c == 0 else ROWS, 1)
        if isinstance(c, int) and c == STEPS + 1:
            return pl.ds(2 + STEP * (c - 2), STEP - 2)
        return pl.ds(2 + STEP * (c - 2), STEP)

    def first_hop(c):
        rows = rows_of(c)
        return [
            pltpu.make_async_remote_copy(
                src_ref=ext.at[rows, pl.ds(start, HALO)],
                dst_ref=buf.at[rows],
                send_sem=s1_send.at[side, c],
                recv_sem=s1_recv.at[side, c],
                device_id=partner,
                device_id_type=MESH,
            )
            for side, (buf, start) in enumerate(((raw_l, HALO), (raw_r, SLOTS)))
        ]

    def second_hop(c):
        rows = rows_of(c)
        return [
            pltpu.make_async_remote_copy(
                src_ref=buf.at[rows],
                dst_ref=ext.at[rows, pl.ds(start, HALO)],
                send_sem=s2_send.at[side, c],
                recv_sem=s2_recv.at[side, c],
                device_id=target,
                device_id_type=MESH,
            )
            for side, (buf, start, target) in enumerate(
                ((raw_l, HALO + SLOTS, to_west), (raw_r, 0, to_east))
            )
        ]

    def features_hop(c):
        rows = pl.ds(STEP * c, STEP)
        return pltpu.make_async_remote_copy(
            src_ref=mid_out.at[rows],
            dst_ref=mid_in.at[rows],
            send_sem=f_send.at[c],
            recv_sem=f_recv.at[c],
            device_id=partner,
            device_id_type=MESH,
        )

    def lat_hop(side):
        src, dst, target = ((1, ROWS + 1, to_north), (ROWS, 0, to_south))[side]
        return pltpu.make_async_remote_copy(
            src_ref=ext.at[src],
            dst_ref=ext.at[dst],
            send_sem=lat_send.at[side],
            recv_sem=lat_recv.at[side],
            device_id=target,
            device_id_type=MESH,
        )

    slot = lax.broadcasted_iota(jnp.int32, (SLOTS, 3 * EXT), 0)
    pos = lax.broadcasted_iota(jnp.int32, (SLOTS, 3 * EXT), 1)
    slot_col = jnp.where(slot < 32, slot, slot - 3)
    for dy in range(3):
        at = pos - EXT * dy
        col = jnp.where(at < HALO + 29, at - HALO, at - HALO - 3)
        good = (at >= 0) & (at < EXT) & ((at < HALO + 29) | (at >= HALO + 32))
        diff[dy] = jnp.where(good, col - slot_col, 1000)

    q_col = lax.broadcasted_iota(jnp.int32, (SLOTS, COLS), 0)
    q_col = jnp.where(q_col < 32, q_col, q_col - 3)
    to_slot = (q_col == lax.broadcasted_iota(jnp.int32, (SLOTS, COLS), 1)).astype(jnp.bfloat16)
    wet_q[...] = jnp.dot(
        to_slot,
        wet_ref[...].astype(jnp.float32).astype(jnp.bfloat16),
        preferred_element_type=jnp.float32,
    ).astype(jnp.bfloat16)

    def silu(v):
        return v * (0.5 + 0.5 * jnp.tanh(0.5 * v))

    def compute(c):
        base = c * STEP

        @pl.loop(0, STEP)
        def _(i):
            window = ext[pl.ds(base + i, 3)].reshape(3 * EXT, C)
            select = jnp.concatenate(
                [
                    jnp.where(diff[t // 3] == off_ref[t // 3, t % 3, base + i], 1.0, 0.0).astype(jnp.bfloat16)
                    for t in range(TAPS)
                ],
                axis=0,
            )
            picked = jnp.dot(select, window, preferred_element_type=jnp.float32).astype(jnp.bfloat16)
            start = pl.multiple_of(i * SLOTS, 16)
            for t in range(TAPS):
                picks[pl.ds(start, SLOTS), t * C : (t + 1) * C] = picked[t * SLOTS : (t + 1) * SLOTS]

        cells = STEP * SLOTS
        acc = jnp.dot(picks[...], cw_ref[...], preferred_element_type=jnp.float32)

        rows = lax.broadcasted_iota(jnp.int32, (ROWS, STEP * K), 0)
        lanes = lax.broadcasted_iota(jnp.int32, (ROWS, STEP * K), 1)
        spread = (rows == base + lanes // K).astype(jnp.bfloat16)
        wet = jnp.dot(wet_q[...], spread, preferred_element_type=jnp.float32)
        wet = jnp.concatenate([wet[:, i * K : (i + 1) * K] for i in range(STEP)], axis=0)
        keep_own = jnp.where(sec == 0, 1.0, wet)
        keep_other = jnp.where(sec == 0, wet, 1.0)

        edge = jnp.concatenate(
            [raw_l[pl.ds(base + 1, STEP)], raw_r[pl.ds(base + 1, STEP)]], axis=1
        ).reshape(STEP * 2 * HALO, C)
        edge = silu(jnp.dot(edge, cp_ref[other], preferred_element_type=jnp.float32))
        edge = edge.reshape(STEP, 2 * HALO, K)
        mid = mid_in[pl.ds(base, STEP)].astype(jnp.float32)
        feat = jnp.concatenate([edge[:, :HALO], mid, edge[:, HALO:]], axis=1).reshape(cells, K)
        feat = (feat * keep_other).astype(jnp.bfloat16)
        pre = acc + jnp.dot(feat, ci_ref[...], preferred_element_type=jnp.float32)

        meansq = jnp.mean(pre * pre, axis=-1, keepdims=True)
        normed = (pre * lax.rsqrt(meansq + 1e-05) * gain_ref[...]).astype(jnp.bfloat16)
        h = jnp.dot(normed, up_ref[...], preferred_element_type=jnp.float32)
        h = 0.5 * h * (1.0 + jnp.tanh(math.sqrt(2.0 / math.pi) * (h + 0.044715 * (h * h * h))))
        update = jnp.dot(h.astype(jnp.bfloat16), down_ref[...], preferred_element_type=jnp.float32)
        update = update * jnp.concatenate([keep_own, keep_own], axis=1)
        field = ext[pl.ds(base + 1, STEP), HALO : HALO + SLOTS].astype(jnp.float32)
        out_ref[pl.ds(base, STEP)] = (field + update.reshape(STEP, SLOTS, C)).astype(jnp.bfloat16)

    load.wait()
    pl.semaphore_wait(barrier, 5)

    def start(copies):
        for copy in copies:
            copy.start()

    for c in range(STEPS + 2):
        start(first_hop(c))

    @pl.loop(0, STEPS)
    def _(c):
        own = ext[pl.ds(c * STEP + 1, STEP), 2 * HALO : 3 * HALO].reshape(STEP * HALO, C)
        own = silu(jnp.dot(own, cp_ref[sec], preferred_element_type=jnp.float32))
        mid_out[pl.ds(c * STEP, STEP)] = own.astype(jnp.bfloat16).reshape(STEP, HALO, K)
        features_hop(c).start()

    def relay(c):
        for arrived, onward in zip(first_hop(c), second_hop(c)):
            arrived.wait_recv()
            onward.start()

    def halo_wait(c):
        for copy in second_hop(c):
            copy.wait_recv()

    relay(0)
    relay(1)
    relay(2)
    halo_wait(0)
    halo_wait(1)
    lat_hop(0).start()
    lat_hop(1).start()

    @pl.loop(0, STEPS)
    def _(c):
        @pl.when(c < STEPS - 2)
        def _():
            relay(c + 3)

        @pl.when(c == STEPS - 2)
        def _():
            relay(STEPS + 1)

        @pl.when(c < STEPS - 1)
        def _():
            halo_wait(c + 2)

        @pl.when(c == STEPS - 1)
        def _():
            halo_wait(STEPS + 1)
            lat_hop(0).wait_recv()

            @pl.when(la == n_lat - 1)
            def _():
                ext[ROWS + 1] = jnp.zeros((EXT, C), jnp.bfloat16)

        @pl.when(c == 0)
        def _():
            lat_hop(1).wait_recv()

            @pl.when(la == 0)
            def _():
                ext[0] = jnp.zeros((EXT, C), jnp.bfloat16)

        features_hop(c).wait_recv()
        compute(c)

    for c in range(STEPS + 2):
        for copy in first_hop(c) + second_hop(c):
            copy.wait_send()
    for c in range(STEPS):
        features_hop(c).wait_send()
    lat_hop(0).wait_send()
    lat_hop(1).wait_send()


def local(state, wet_mask, tap_offsets, conv_weight, couple_proj, couple_in, norm_gain, up_weight, down_weight):
    x = state[0]
    x = jnp.concatenate([x[:, :32], x[:, 29:]], axis=1)
    vmem = pl.BlockSpec(memory_space=pltpu.VMEM)
    dma = pltpu.SemaphoreType.DMA
    out = pl.pallas_call(
        kernel,
        out_shape=jax.ShapeDtypeStruct((ROWS, SLOTS, C), jnp.bfloat16),
        in_specs=[pl.BlockSpec(memory_space=pl.ANY), vmem, pl.BlockSpec(memory_space=pltpu.SMEM)] + [vmem] * 6,
        out_specs=vmem,
        scratch_shapes=[
            pltpu.VMEM((ROWS + 2, EXT, C), jnp.bfloat16),
            pltpu.VMEM((ROWS + 2, HALO, C), jnp.bfloat16),
            pltpu.VMEM((ROWS + 2, HALO, C), jnp.bfloat16),
            pltpu.VMEM((ROWS, HALO, K), jnp.bfloat16),
            pltpu.VMEM((ROWS, HALO, K), jnp.bfloat16),
            pltpu.VMEM((3, SLOTS, 3 * EXT), jnp.int32),
            pltpu.VMEM((SLOTS, ROWS), jnp.bfloat16),
            pltpu.VMEM((STEP * SLOTS, TAPS * C), jnp.bfloat16),
            dma,
            dma((2, STEPS + 2)),
            dma((2, STEPS + 2)),
            dma((2, STEPS + 2)),
            dma((2, STEPS + 2)),
            dma((STEPS,)),
            dma((STEPS,)),
            dma((2,)),
            dma((2,)),
        ],
        compiler_params=pltpu.CompilerParams(
            collective_id=0, has_side_effects=True, vmem_limit_bytes=48 * 1024 * 1024
        ),
        cost_estimate=pl.CostEstimate(flops=8_000_000_000, bytes_accessed=5_000_000, transcendentals=2_000_000),
    )(
        x,
        wet_mask.T,
        tap_offsets.transpose(1, 2, 0),
        conv_weight[0].reshape(TAPS * C, C),
        couple_proj,
        couple_in[0],
        norm_gain,
        up_weight[0],
        down_weight[0],
    )
    return jnp.concatenate([out[:, :29], out[:, 32:]], axis=1)[None]


def solution(mesh):
    in_specs = (
        P("sec", "lat", "lon", None),
        P("lat", "lon"),
        P("lat", None, None),
        P("sec", None, None, None),
        P(),
        P("sec", None, None),
        P("sec", None),
        P("sec", None, None),
        P("sec", None, None),
    )
    out_specs = P("sec", "lat", "lon", None)
    return jax.shard_map(local, mesh=mesh, in_specs=in_specs, out_specs=out_specs, check_vma=False)
```

time: 123 us -> 77.8 us (0.63)
  the two profiles are of different devices: /device:TPU:7 before, /device:TPU:24 now
where the time goes in v1:
time: 77.8 us; the launch traced here: 77.6 us
  Pallas kernels  71.4 us (92%)
  local copies, waits for them, and re-layouts  5.55 us (7%)
    pallas_call x1, Pallas kernels, local(): pl.pallas_call(kernel, out_shape=jax.ShapeDtypeStruct((ROWS, SLOTS, C), j...  71.4 us
    unnamed x17, local copies, waits for them, and re-layouts  3.45 us
    broadcast_in_dim x1, local copies, waits for them, and re-layouts, local(): return jnp.concatenate([out[:, :29], out[:, 32:]], axis=1)[None]  1.61 us

profile of v1, /device:TPU:24, one launch (start us, length us, event | category | flops | bytes accessed | tf_op | source)
XLA Modules:
  0.0 77.6 jit_solution(16870754379045003938)
XLA Ops:
  0.0 2.2 %copy.13 = bf16[1,64,45,256]{3,2,1,0:T(8,128)(2,1)S(1)} copy(bf16[1,64,45,256]{3,1,2,0:T(8,128)(2,1)} %param.9) | data formatting | bytes 2949120 | tf_op args[0]
  2.2 0.2 slice.17
  2.4 0.1 slice.16
  2.6 0.0 copy-start
  2.6 0.0 copy-start.1
  2.6 0.0 copy-start.2
  2.6 0.0 copy-start.3
  2.6 0.0 copy-start.4
  2.6 0.0 copy-start.5
  2.6 0.0 copy-start.6
  2.6 0.0 copy-start.7
  2.7 0.1 pad_maximum_fusion.x_ref
  2.8 1.1 %copy-done = bf16[1,9,256,256]{3,2,1,0:T(8,128)(2,1)S(1)} copy-done((bf16[1,9,256,256]{3,2,1,0:T(8,128)(2,1)S(1)}, bf16[1,9,256,256]{3,2,1,0:T(8,128)(2,1)}, u32[]{:S(2)}) %copy-start) | copy-done | bytes 1179672
  3.8 0.0 copy-done.1
  3.9 0.1 copy-done.2
  3.9 0.0 copy-done.3
  4.0 0.0 copy-done.4
  4.0 0.0 copy-done.5
  4.0 0.0 copy-done.6
  4.0 0.0 copy-done.7
  4.0 71.4 %shard_map.91 = bf16[64,48,256]{2,1,0:T(8,128)(2,1)S(1)} custom-call(bf16[64,48,256]{2,1,0:T(8,128)(2,1)S(1)} %pad_maximum_fusion.x_ref, s32[45,64]{1,0:T(8,128)S(1)} %bitcast.15, s32[3,3,64]{2,1,0:T(4,128)S(1)} %bitcast.16, bf16[2304,256]{1,0:T(8,128)(2,1)S(1)} %bitcast.11, bf16[2,256,128]{2,1,0:T(8,128)(2,1)S(1)} %copy-done.3, ...), custom_call_target="tpu_custom_call" | custom-call | flops 8000000000 | bytes 5000000 | tf_op jit(solution)/shard_map/pallas_call | solution.py:285
  75.5 0.1 slice.14
  75.6 0.4 maximum_bitcast_fusion
  76.0 1.6 %copy.11 = bf16[1,64,45,256]{3,1,2,0:T(8,128)(2,1)} copy(bf16[1,64,45,256]{3,2,1,0:T(8,128)(2,1)S(1)} %maximum_bitcast_fusion) | data formatting | bytes 2949120 | tf_op jit(solution)/shard_map/broadcast_in_dim | solution.py:324
  (1 shorter events, 0.0 us)
Async XLA Ops:
  2.6 1.3 %copy-start = (bf16[1,9,256,256]{3,2,1,0:T(8,128)(2,1)S(1)}, bf16[1,9,256,256]{3,2,1,0:T(8,128)(2,1)}, u32[]{:S(2)}) copy-start(bf16[1,9,256,256]{3,2,1,0:T(8,128)(2,1)} %param.12) | copy-start | bytes 3538948
  2.6 1.3 %copy-start.1 = (bf16[1,256,512]{2,1,0:T(8,128)(2,1)S(1)}, bf16[1,256,512]{2,1,0:T(8,128)(2,1)}, u32[]{:S(2)}) copy-start(bf16[1,256,512]{2,1,0:T(8,128)(2,1)} %param.16) | copy-start | bytes 786436
  2.6 1.4 %copy-start.2 = (bf16[1,512,256]{2,1,0:T(8,128)(2,1)S(1)}, bf16[1,512,256]{2,1,0:T(8,128)(2,1)}, u32[]{:S(2)}) copy-start(bf16[1,512,256]{2,1,0:T(8,128)(2,1)} %param.17) | copy-start | bytes 786436
  2.6 1.4 %copy-start.3 = (bf16[2,256,128]{2,1,0:T(8,128)(2,1)S(1)}, bf16[2,256,128]{2,1,0:T(8,128)(2,1)}, u32[]{:S(2)}) copy-start(bf16[2,256,128]{2,1,0:T(8,128)(2,1)} %cp_ref.1) | copy-start | bytes 393220
  2.6 1.4 %copy-start.4 = (bf16[1,128,256]{2,1,0:T(8,128)(2,1)S(1)}, bf16[1,128,256]{2,1,0:T(8,128)(2,1)}, u32[]{:S(2)}) copy-start(bf16[1,128,256]{2,1,0:T(8,128)(2,1)} %param.14) | copy-start | bytes 196612
  2.6 1.4 %copy-start.5 = (s32[64,45]{0,1:T(8,128)S(1)}, s32[64,45]{0,1:T(8,128)}, u32[]{:S(2)}) copy-start(s32[64,45]{0,1:T(8,128)} %param.10) | copy-start | bytes 34564
  2.6 1.4 %copy-start.6 = (s32[64,3,3]{0,2,1:T(4,128)S(1)}, s32[64,3,3]{0,2,1:T(4,128)}, u32[]{:S(2)}) copy-start(s32[64,3,3]{0,2,1:T(4,128)} %param.11) | copy-start | bytes 6916
  2.6 1.3 %copy-start.7 = (f32[1,256]{1,0:T(1,128)S(1)}, f32[1,256]{1,0:T(1,128)}, u32[]{:S(2)}) copy-start(f32[1,256]{1,0:T(1,128)} %gain_ref.1) | copy-start | bytes 3076

commit v2 on v1

v2 whole, which is shorter than its diff:
```python
import math

import jax
import jax.numpy as jnp
from jax import lax
from jax.experimental import pallas as pl
from jax.experimental.pallas import tpu as pltpu
from jax.sharding import PartitionSpec as P

HALO = 16
ROWS = 64
COLS = 45
SLOTS = 48
EXT = 82
C = 256
K = 128
HID = 512
STEP = 8
STEPS = ROWS // STEP
CHUNKS = STEPS + 2
AHEAD = 2
LEAD = 4
COL_UNROLL = 5
GROUP = 16
TAPS = 9
MESH = pl.DeviceIdType.MESH


def kernel(
    x_hbm,
    wet_hbm,
    off_hbm,
    cw_hbm,
    cp_hbm,
    ci_hbm,
    gain_hbm,
    up_hbm,
    down_hbm,
    out_ref,
    x_ref,
    wet_ref,
    off_ref,
    cw_ref,
    cp_ref,
    ci_ref,
    gain_ref,
    up_ref,
    down_ref,
    wide,
    own_l,
    own_m,
    own_r,
    raw_l,
    raw_r,
    halo_l,
    halo_r,
    lat_out,
    lat_in,
    mid_out,
    mid_in,
    feat,
    wet_q,
    picks,
    load_sem,
    s1_send,
    s1_recv,
    s2_send,
    s2_recv,
    f_send,
    f_recv,
    lat_send,
    lat_recv,
):
    sec = lax.axis_index("sec")
    la = lax.axis_index("lat")
    lo = lax.axis_index("lon")
    n_lat = lax.axis_size("lat")
    n_lon = lax.axis_size("lon")
    other = 1 - sec
    west, east = lax.rem(lo + n_lon - 1, n_lon), lax.rem(lo + 1, n_lon)
    north, south = lax.rem(la + n_lat - 1, n_lat), lax.rem(la + 1, n_lat)
    partner = (other, la, lo)
    to_west = (other, la, west)
    to_east = (other, la, east)
    to_north = (sec, north, lo)
    to_south = (sec, south, lo)

    barrier = pltpu.get_barrier_semaphore()
    for peer in (partner, to_west, to_east, to_north, to_south):
        pl.semaphore_signal(barrier, inc=1, device_id=peer, device_id_type=MESH)

    loads = [
        pltpu.make_async_copy(src, dst, load_sem.at[i])
        for i, (src, dst) in enumerate(
            (
                (x_hbm, x_ref),
                (cp_hbm, cp_ref),
                (wet_hbm, wet_ref),
                (off_hbm, off_ref),
                (ci_hbm, ci_ref),
                (gain_hbm, gain_ref),
                (cw_hbm, cw_ref),
                (up_hbm, up_ref),
                (down_hbm, down_ref),
            )
        )
    ]
    for copy in loads:
        copy.start()

    def rows_of(c):
        if isinstance(c, int) and c < 2:
            return pl.ds(1 if c == 0 else ROWS, 1)
        if isinstance(c, int) and c == CHUNKS - 1:
            return pl.ds(2 + STEP * (c - 2), STEP - 2)
        return pl.ds(2 + STEP * (c - 2), STEP)

    def hop(c, pairs, targets, send_sem, recv_sem):
        rows = rows_of(c)
        return [
            pltpu.make_async_remote_copy(
                src_ref=src.at[rows],
                dst_ref=dst.at[rows],
                send_sem=send_sem.at[side, c],
                recv_sem=recv_sem.at[side, c],
                device_id=targets[side],
                device_id_type=MESH,
            )
            for side, (src, dst) in enumerate(pairs)
        ]

    def first_hop(c):
        return hop(c, ((own_l, raw_l), (own_r, raw_r)), (partner, partner), s1_send, s1_recv)

    def second_hop(c):
        return hop(c, ((raw_l, halo_r), (raw_r, halo_l)), (to_west, to_east), s2_send, s2_recv)

    def features_hop(c):
        rows = pl.ds(STEP * c, STEP)
        return pltpu.make_async_remote_copy(
            src_ref=mid_out.at[rows],
            dst_ref=mid_in.at[rows],
            send_sem=f_send.at[c],
            recv_sem=f_recv.at[c],
            device_id=partner,
            device_id_type=MESH,
        )

    def lat_hop(side):
        return pltpu.make_async_remote_copy(
            src_ref=lat_out.at[side],
            dst_ref=lat_in.at[side],
            send_sem=lat_send.at[side],
            recv_sem=lat_recv.at[side],
            device_id=(to_north, to_south)[side],
            device_id_type=MESH,
        )

    def silu(v):
        return v * (0.5 + 0.5 * jnp.tanh(0.5 * v))

    def at(row, half, col):
        return (row * 2 + half) * EXT + col

    halves = [slice(half * 128, half * 128 + 128) for half in range(2)]

    def to_rows(g):
        base = g * GROUP

        @pl.loop(0, COLS, unroll=COL_UNROLL)
        def _(col):
            x = x_ref[col, pl.ds(pl.multiple_of(base, GROUP), GROUP)].astype(jnp.float32)
            for half in range(2):
                wide[pl.ds(at(base + 1, half, HALO + col), GROUP, 2 * EXT), :] = x[:, halves[half]]

        @pl.loop(0, GROUP, unroll=2)
        def _(i):
            row = base + 1 + i
            for half in range(2):
                for dst, col in ((own_l, 0), (own_m, 16), (own_r, COLS - HALO)):
                    dst[row, :, halves[half]] = wide[pl.ds(at(row, half, HALO + col), HALO), :].astype(jnp.bfloat16)

    def widen(start, rows):
        for row in range(rows):
            for half in range(2):
                for src, col in ((halo_l, 0), (halo_r, HALO + COLS)):
                    x = src[start + row, :, halves[half]]
                    wide[pl.ds(at(start + row, half, col), HALO), :] = x.astype(jnp.float32)

    def start(copies):
        for copy in copies:
            copy.start()

    def relay(c):
        for arrived, onward in zip(first_hop(c), second_hop(c)):
            arrived.wait_recv()
            onward.start()

    def sent(c):
        for copy in first_hop(c):
            copy.wait_send()

    def pass_on(c):
        relay(c)
        sent(c)
        start(first_hop(c + AHEAD))

    def halo_wait(c):
        for copy in second_hop(c):
            copy.wait_recv()

    def lat_row(side, real):
        row = (ROWS + 1, 0)[side]
        for half in range(2):
            x = lat_in[side, 0:EXT, halves[half]].astype(jnp.float32)
            wide[pl.ds(at(row, half, 0), EXT), :] = jnp.where(real, x, 0.0)

    def compute(c):
        base = c * STEP
        cells = STEP * SLOTS

        @pl.loop(0, STEP)
        def _(i):
            start = pl.multiple_of(i * SLOTS, 16)
            for t in range(TAPS):
                first = off_ref[t // 3, t % 3, base + i] + HALO
                for half in range(2):
                    picked = wide[pl.ds(at(base + i + t // 3, half, first), SLOTS), :]
                    lanes = slice(t * C + half * 128, t * C + half * 128 + 128)
                    picks[pl.ds(start, SLOTS), lanes] = picked.astype(jnp.bfloat16)

        acc = jnp.dot(picks[...], cw_ref[...], preferred_element_type=jnp.float32)

        rows = lax.broadcasted_iota(jnp.int32, (ROWS, STEP * K), 0)
        lanes = lax.broadcasted_iota(jnp.int32, (ROWS, STEP * K), 1)
        spread = (rows == base + lanes // K).astype(jnp.bfloat16)
        wet = jnp.dot(wet_q[...], spread, preferred_element_type=jnp.float32)
        wet = jnp.concatenate([wet[:, i * K : (i + 1) * K] for i in range(STEP)], axis=0)
        keep_own = jnp.where(sec == 0, 0.5, 0.5 * wet)
        keep_other = jnp.where(sec == 0, wet, 1.0)

        edge = jnp.concatenate(
            [raw_l[pl.ds(base + 1, STEP)], raw_r[pl.ds(base + 1, STEP)]], axis=1
        ).reshape(STEP * 2 * HALO, C)
        edge = silu(jnp.dot(edge, cp_ref[other], preferred_element_type=jnp.float32))
        edge = edge.reshape(STEP, 2 * HALO, K)
        feat[:, 0:16] = edge[:, :HALO]
        feat[:, 16:32] = mid_in[pl.ds(base, STEP)].astype(jnp.float32)
        feat[:, 29:45] = edge[:, HALO:]
        coupled = (feat[...].reshape(cells, K) * keep_other).astype(jnp.bfloat16)
        pre = acc + jnp.dot(coupled, ci_ref[...], preferred_element_type=jnp.float32)

        meansq = jnp.mean(pre * pre, axis=-1, keepdims=True)
        normed = (pre * lax.rsqrt(meansq + 1e-05) * gain_ref[...]).astype(jnp.bfloat16)
        h = jnp.dot(normed, up_ref[...], preferred_element_type=jnp.float32)
        s2p = math.sqrt(2.0 / math.pi)
        h = h + h * jnp.tanh(h * (s2p + (s2p * 0.044715) * (h * h)))
        update = jnp.dot(h.astype(jnp.bfloat16), down_ref[...], preferred_element_type=jnp.float32)
        update = update * jnp.concatenate([keep_own, keep_own], axis=1)
        field = [
            jnp.concatenate([wide[pl.ds(at(base + 1 + i, half, HALO), SLOTS), :] for i in range(STEP)], axis=0)
            for half in range(2)
        ]
        result = (jnp.concatenate(field, axis=1) + update).reshape(STEP, SLOTS, C)
        out_ref[pl.ds(base, STEP)] = result[:, :COLS].astype(jnp.bfloat16)

    loads[0].wait()
    last = ROWS // GROUP - 1
    to_rows(0)
    to_rows(last)
    pl.semaphore_wait(barrier, 5)
    for c in range(2 + min(AHEAD, GROUP // STEP - 1)):
        start(first_hop(c))

    @pl.loop(1, last)
    def _(g):
        to_rows(g)

    for c in range(2 + min(AHEAD, GROUP // STEP - 1), 2 + AHEAD):
        start(first_hop(c))

    loads[1].wait()

    @pl.loop(0, ROWS // GROUP)
    def _(g):
        own = own_m[pl.ds(g * GROUP + 1, GROUP)].reshape(GROUP * HALO, C)
        own = silu(jnp.dot(own, cp_ref[sec], preferred_element_type=jnp.float32))
        mid_out[pl.ds(g * GROUP, GROUP)] = own.astype(jnp.bfloat16).reshape(GROUP, HALO, K)

    features_hop(0).start()

    loads[2].wait()
    to_slot = lax.broadcasted_iota(jnp.int32, (SLOTS, COLS), 0) == lax.broadcasted_iota(jnp.int32, (SLOTS, COLS), 1)
    wet_q[...] = jnp.dot(
        to_slot.astype(jnp.bfloat16),
        wet_ref[...].astype(jnp.float32).astype(jnp.bfloat16),
        preferred_element_type=jnp.float32,
    ).astype(jnp.bfloat16)
    feat[...] = jnp.zeros_like(feat)

    @pl.loop(0, (ROWS + 2) * 2)
    def _(i):
        wide[pl.ds(i * EXT + 77, 5), :] = jnp.zeros((5, 128), jnp.float32)

    for copy in loads[3:]:
        copy.wait()

    relay(0)
    relay(1)
    pass_on(2)
    halo_wait(0)
    halo_wait(1)
    for side, row in enumerate((1, ROWS)):
        widen(row, 1)
        for half in range(2):
            lat_out[side, 0:EXT, halves[half]] = wide[pl.ds(at(row, half, 0), EXT), :].astype(jnp.bfloat16)
        lat_hop(side).start()
    for c in range(3, LEAD):
        pass_on(c)

    @pl.loop(0, STEPS)
    def _(c):
        @pl.when(c < CHUNKS - 1 - LEAD)
        def _():
            relay(c + LEAD)
            sent(c + LEAD)

        @pl.when(c < CHUNKS - 1 - LEAD - AHEAD)
        def _():
            start(first_hop(c + LEAD + AHEAD))

        @pl.when(c == CHUNKS - 1 - LEAD - AHEAD)
        def _():
            start(first_hop(CHUNKS - 1))

        @pl.when(c < STEPS - 1)
        def _():
            features_hop(c + 1).start()

        @pl.when(c == CHUNKS - 1 - LEAD)
        def _():
            relay(CHUNKS - 1)
            sent(CHUNKS - 1)

        @pl.when(c < STEPS - 1)
        def _():
            halo_wait(c + 2)
            widen(STEP * c + 2, STEP)

        @pl.when(c == STEPS - 1)
        def _():
            halo_wait(CHUNKS - 1)
            widen(2 + STEP * (STEPS - 1), STEP - 2)
            lat_hop(0).wait_recv()
            lat_row(0, la < n_lat - 1)

        @pl.when(c == 0)
        def _():
            lat_hop(1).wait_recv()
            lat_row(1, la > 0)

        features_hop(c).wait_recv()
        compute(c)

    sent(0)
    sent(1)
    for c in range(CHUNKS):
        for copy in second_hop(c):
            copy.wait_send()
    for c in range(STEPS):
        features_hop(c).wait_send()
    lat_hop(0).wait_send()
    lat_hop(1).wait_send()


def local(state, wet_mask, tap_offsets, conv_weight, couple_proj, couple_in, norm_gain, up_weight, down_weight):
    args = (
        state[0].transpose(1, 0, 2),
        wet_mask.T,
        tap_offsets.transpose(1, 2, 0),
        conv_weight[0].reshape(TAPS * C, C),
        couple_proj,
        couple_in[0],
        norm_gain,
        up_weight[0],
        down_weight[0],
    )
    dma = pltpu.SemaphoreType.DMA
    edge = pltpu.VMEM((ROWS + 2, HALO, C), jnp.bfloat16)
    out = pl.pallas_call(
        kernel,
        out_shape=jax.ShapeDtypeStruct((ROWS, COLS, C), jnp.bfloat16),
        in_specs=[pl.BlockSpec(memory_space=pltpu.HBM)] * len(args),
        out_specs=pl.BlockSpec(memory_space=pltpu.VMEM),
        scratch_shapes=[(pltpu.SMEM if i == 2 else pltpu.VMEM)(a.shape, a.dtype) for i, a in enumerate(args)]
        + [
            pltpu.VMEM(((ROWS + 2) * 2 * EXT, 128), jnp.float32),
        ]
        + [edge] * 7
        + [
            pltpu.VMEM((2, 96, C), jnp.bfloat16),
            pltpu.VMEM((2, 96, C), jnp.bfloat16),
            pltpu.VMEM((ROWS, HALO, K), jnp.bfloat16),
            pltpu.VMEM((ROWS, HALO, K), jnp.bfloat16),
            pltpu.VMEM((STEP, SLOTS, K), jnp.float32),
            pltpu.VMEM((SLOTS, ROWS), jnp.bfloat16),
            pltpu.VMEM((STEP * SLOTS, TAPS * C), jnp.bfloat16),
            dma((len(args),)),
            dma((2, CHUNKS)),
            dma((2, CHUNKS)),
            dma((2, CHUNKS)),
            dma((2, CHUNKS)),
            dma((STEPS,)),
            dma((STEPS,)),
            dma((2,)),
            dma((2,)),
        ],
        compiler_params=pltpu.CompilerParams(
            collective_id=0, has_side_effects=True, vmem_limit_bytes=62 * 1024 * 1024
        ),
        cost_estimate=pl.CostEstimate(flops=6_000_000_000, bytes_accessed=5_000_000, transcendentals=2_000_000),
    )(*args)
    return out[None]


def solution(mesh):
    in_specs = (
        P("sec", "lat", "lon", None),
        P("lat", "lon"),
        P("lat", None, None),
        P("sec", None, None, None),
        P(),
        P("sec", None, None),
        P("sec", None),
        P("sec", None, None),
        P("sec", None, None),
    )
    out_specs = P("sec", "lat", "lon", None)
    return jax.shard_map(local, mesh=mesh, in_specs=in_specs, out_specs=out_specs, check_vma=False)
```

time: 77.8 us -> 55.5 us (0.71)
  Pallas kernels: 71.4 us -> 52.4 us
  local copies, waits for them, and re-layouts: 5.55 us -> 3.02 us
    pallas_call x1, Pallas kernels: 71.4 us -> 52.4 us  [local(): pl.pallas_call(kernel, out_shape=jax.ShapeDtypeStruct((ROWS, COLS, C), jn...]
    unnamed x17 -> x0, local copies, waits for them, and re-layouts: 3.45 us -> none
    broadcast_in_dim x1, local copies, waits for them, and re-layouts: 1.61 us -> 3.02 us  [local(): return out[None]]
where the time goes in v2:
time: 55.5 us; the launch traced here: 55.4 us
  Pallas kernels  52.4 us (94%)
  local copies, waits for them, and re-layouts  3.02 us (5%)
    pallas_call x1, Pallas kernels, local(): pl.pallas_call(kernel, out_shape=jax.ShapeDtypeStruct((ROWS, COLS, C), jn...  52.4 us
    broadcast_in_dim x1, local copies, waits for them, and re-layouts, local(): return out[None]  3.02 us

profile of v2, /device:TPU:24, one launch (start us, length us, event | category | flops | bytes accessed | tf_op | source)
XLA Modules:
  0.0 55.4 jit_solution(3521796316809260117)
XLA Ops:
  0.0 52.4 %shard_map.91 = bf16[64,45,256]{2,1,0:T(8,128)(2,1)} custom-call(bf16[45,64,256]{2,1,0:T(8,128)(2,1)} %bitcast.11, s32[45,64]{1,0:T(8,128)} %bitcast.16, s32[3,3,64]{2,1,0:T(4,128)} %bitcast.17, bf16[2304,256]{1,0:T(8,128)(2,1)} %bitcast.12, bf16[2,256,128]{2,1,0:T(8,128)(2,1)} %cp_hbm.1, bf16[128,256]{1,0:T(8,128)(2,1)} %bitcast.15, f32[1,256]{1,0:T(1,128)} %gain_hbm.1, ...), custom_call_target="tpu_custom_call" | custom-call | flops 6000000000 | bytes 5000000 | tf_op jit(solution)/shard_map/pallas_call | solution.py:390
  52.4 3.0 %copy.10 = bf16[1,64,45,256]{3,1,2,0:T(8,128)(2,1)} copy(bf16[1,64,45,256]{3,2,1,0:T(8,128)(2,1)} %bitcast.10) | data formatting | bytes 2949120 | tf_op jit(solution)/shard_map/broadcast_in_dim | solution.py:423

commit v3 on v2

v3 whole, which is shorter than its diff:
```python
import math

import jax
import jax.numpy as jnp
from jax import lax
from jax.experimental import pallas as pl
from jax.experimental.pallas import tpu as pltpu
from jax.sharding import PartitionSpec as P

HALO = 16
ROWS = 64
COLS = 45
EXT = 82
C = 256
K = 128
HID = 512
STEP = 16
STEPS = ROWS // STEP
CHUNKS = STEPS + 2
WIDE = 32
EARLY = 4
LEAD = 4
COL_UNROLL = 5
TAPS = 9
MESH = pl.DeviceIdType.MESH


def kernel(
    x_hbm,
    wet_hbm,
    off_hbm,
    cw_hbm,
    cp_hbm,
    ci_hbm,
    gain_hbm,
    up_hbm,
    down_hbm,
    out_ref,
    x_ref,
    wet_ref,
    off_ref,
    cw_ref,
    cp_ref,
    ci_ref,
    gain_ref,
    up_ref,
    down_ref,
    wide,
    own_far,
    own_mid,
    own_near,
    raw_far,
    raw_near,
    halo_far,
    halo_near,
    lat_out,
    lat_in,
    mid_out,
    mid_in,
    feat,
    wet_far,
    wet_near,
    picks,
    load_sem,
    far_sem,
    near_sem,
    hello,
    f_send,
    f_recv,
    lat_send,
    lat_recv,
):
    sec = lax.axis_index("sec")
    la = lax.axis_index("lat")
    lo = lax.axis_index("lon")
    n_lat = lax.axis_size("lat")
    n_lon = lax.axis_size("lon")
    other = 1 - sec
    odd = lax.rem(lo, 2)
    near = lo + 1 - 2 * odd
    far = lax.rem(lo + n_lon - 1 + 2 * odd, n_lon)
    north, south = lax.rem(la + n_lat - 1, n_lat), lax.rem(la + 1, n_lat)
    partner = (other, la, lo)
    to_near = (other, la, near)
    to_far = (other, la, far)
    to_north = (sec, north, lo)
    to_south = (sec, south, lo)

    barrier = pltpu.get_barrier_semaphore()

    def tell(*peers):
        for peer in peers:
            pl.semaphore_signal(barrier, inc=1, device_id=peer, device_id_type=MESH)

    def greet(i, peer):
        pl.semaphore_signal(hello.at[i], inc=1, device_id=peer, device_id_type=MESH)

    @pl.when(sec == 0)
    def _():
        tell(to_north, to_south, to_far)

    @pl.when(sec == 1)
    def _():
        tell(partner, to_near, to_north, to_south)

    def meet_far():
        pl.semaphore_wait(barrier, 3)
        greet(2, to_far)

    loads = [
        pltpu.make_async_copy(src, dst, load_sem.at[i])
        for i, (src, dst) in enumerate(
            (
                (x_hbm, x_ref),
                (cp_hbm, cp_ref),
                (wet_hbm, wet_ref),
                (off_hbm, off_ref),
                (ci_hbm, ci_ref),
                (gain_hbm, gain_ref),
                (cw_hbm, cw_ref),
                (up_hbm, up_ref),
                (down_hbm, down_ref),
            )
        )
    ]
    for copy in loads:
        copy.start()

    def rows_of(c):
        if isinstance(c, int) and c < 2:
            return pl.ds(1 if c == 0 else ROWS, 1)
        if isinstance(c, int) and c == CHUNKS - 1:
            return pl.ds(2 + STEP * (c - 2), STEP - 2)
        return pl.ds(2 + STEP * (c - 2), STEP)

    def hop(rows, src, dst, sems, first, c, target):
        return pltpu.make_async_remote_copy(
            src_ref=src.at[rows],
            dst_ref=dst.at[rows],
            send_sem=sems.at[first, c],
            recv_sem=sems.at[first + 1, c],
            device_id=target,
            device_id_type=MESH,
        )

    def far_first(c):
        return hop(rows_of(c), own_far, raw_far, far_sem, 0, c, partner)

    def far_second(c):
        return hop(rows_of(c), raw_far, halo_far, far_sem, 2, c, to_far)

    def near_first(c):
        return hop(rows_of(c), own_near, raw_near, near_sem, 0, c, partner)

    def near_second(c):
        return hop(rows_of(c), raw_near, halo_near, near_sem, 2, c, to_near)

    def features_hop(c):
        rows = pl.ds(STEP * c, STEP)
        return pltpu.make_async_remote_copy(
            src_ref=mid_out.at[rows],
            dst_ref=mid_in.at[rows],
            send_sem=f_send.at[c],
            recv_sem=f_recv.at[c],
            device_id=partner,
            device_id_type=MESH,
        )

    def lat_hop(side):
        return pltpu.make_async_remote_copy(
            src_ref=lat_out.at[side],
            dst_ref=lat_in.at[side],
            send_sem=lat_send.at[side],
            recv_sem=lat_recv.at[side],
            device_id=(to_north, to_south)[side],
            device_id_type=MESH,
        )

    def silu(v):
        return v * (0.5 + 0.5 * jnp.tanh(0.5 * v))

    def at(row, half, col):
        return (row * 2 + half) * EXT + col

    far_col, near_col = (COLS - HALO) * odd, (COLS - HALO) * (1 - odd)
    far_at, near_at = (HALO + COLS) * odd, (HALO + COLS) * (1 - odd)
    halves = [slice(half * 128, half * 128 + 128) for half in range(2)]

    def to_rows(g):
        base = g * STEP

        @pl.loop(0, COLS, unroll=COL_UNROLL)
        def _(col):
            x = x_ref[col, pl.ds(pl.multiple_of(base, STEP), STEP)].astype(jnp.float32)
            for half in range(2):
                wide[pl.ds(at(base + 1, half, HALO + col), STEP, 2 * EXT), :] = x[:, halves[half]]

        @pl.loop(0, STEP, unroll=2)
        def _(i):
            row = base + 1 + i
            for half in range(2):
                for dst, col in ((own_far, far_col), (own_mid, 16), (own_near, near_col)):
                    dst[row, :, halves[half]] = wide[pl.ds(at(row, half, HALO + col), HALO), :].astype(jnp.bfloat16)

    def widen(halo, where, start, rows):
        for row in range(rows):
            for half in range(2):
                x = halo[start + row, :, halves[half]]
                wide[pl.ds(at(start + row, half, where), HALO), :] = x.astype(jnp.float32)

    def relay(arrived, onward):
        arrived.wait_recv()
        onward.start()

    def lat_row(side, real):
        row = (ROWS + 1, 0)[side]
        for half in range(2):
            x = lat_in[side, 0:EXT, halves[half]].astype(jnp.float32)
            wide[pl.ds(at(row, half, 0), EXT), :] = jnp.where(real, x, 0.0)

    def edge_features(raw, base):
        x = raw[pl.ds(base + 1, STEP)].reshape(STEP * HALO, C)
        return silu(jnp.dot(x, cp_ref[other], preferred_element_type=jnp.float32))

    def compute(base, cols, first_col, features, wet_of):
        cells = STEP * cols

        @pl.loop(0, STEP)
        def _(i):
            start = pl.multiple_of(i * cols, 16)
            for t in range(TAPS):
                first = off_ref[t // 3, t % 3, base + i] + HALO + first_col
                for half in range(2):
                    picked = wide[pl.ds(at(base + i + t // 3, half, first), cols), :]
                    lanes = slice(t * C + half * 128, t * C + half * 128 + 128)
                    picks[pl.ds(start, cols), lanes] = picked.astype(jnp.bfloat16)

        acc = jnp.dot(picks[0:cells], cw_ref[...], preferred_element_type=jnp.float32)

        rows = lax.broadcasted_iota(jnp.int32, (ROWS, STEP * K), 0)
        lanes = lax.broadcasted_iota(jnp.int32, (ROWS, STEP * K), 1)
        spread = (rows == base + lanes // K).astype(jnp.bfloat16)
        wet = jnp.dot(wet_of[...], spread, preferred_element_type=jnp.float32)
        wet = jnp.concatenate([wet[:, i * K : (i + 1) * K] for i in range(STEP)], axis=0)
        keep_own = jnp.where(sec == 0, 0.5, 0.5 * wet)
        keep_other = jnp.where(sec == 0, wet, 1.0)

        coupled = (features * keep_other).astype(jnp.bfloat16)
        pre = acc + jnp.dot(coupled, ci_ref[...], preferred_element_type=jnp.float32)
        meansq = jnp.mean(pre * pre, axis=-1, keepdims=True)
        normed = (pre * lax.rsqrt(meansq + 1e-05) * gain_ref[...]).astype(jnp.bfloat16)
        h = jnp.dot(normed, up_ref[...], preferred_element_type=jnp.float32)
        s2p = math.sqrt(2.0 / math.pi)
        h = h + h * jnp.tanh(h * (s2p + (s2p * 0.044715) * (h * h)))
        update = jnp.dot(h.astype(jnp.bfloat16), down_ref[...], preferred_element_type=jnp.float32)
        update = update * jnp.concatenate([keep_own, keep_own], axis=1)
        field = [
            jnp.concatenate(
                [wide[pl.ds(at(base + 1 + i, half, HALO + first_col), cols), :] for i in range(STEP)], axis=0
            )
            for half in range(2)
        ]
        return (jnp.concatenate(field, axis=1) + update).astype(jnp.bfloat16).reshape(STEP, cols, C)

    def compute_far(c):
        base = c * STEP
        rows = pl.ds(base, STEP)
        edge = edge_features(raw_far, base).reshape(STEP, HALO, K)
        mid = mid_in[rows].astype(jnp.float32)
        feat[:, 0:16] = jnp.where(odd == 0, edge, mid)

        @pl.when(odd == 0)
        def _():
            feat[:, 16:32] = mid

        @pl.when(odd == 1)
        def _():
            feat[:, 13:29] = edge

        result = compute(base, WIDE, HALO * odd, feat[...].reshape(STEP * WIDE, K), wet_far)

        @pl.when(odd == 0)
        def _():
            out_ref[rows, 0 : COLS - HALO] = result[:, : COLS - HALO]

        @pl.when(odd == 1)
        def _():
            out_ref[rows, HALO:COLS] = result[:, : COLS - HALO]

    def compute_near(c):
        base = c * STEP
        rows = pl.ds(base, STEP)
        result = compute(base, HALO, near_col, edge_features(raw_near, base), wet_near)

        @pl.when(odd == 0)
        def _():
            out_ref[rows, COLS - HALO : COLS] = result

        @pl.when(odd == 1)
        def _():
            out_ref[rows, 0:HALO] = result

    loads[0].wait()
    last = STEPS - 1
    to_rows(0)
    to_rows(last)

    @pl.when(sec == 0)
    def _():
        pl.semaphore_wait(barrier, 4)
        greet(0, partner)
        greet(1, to_near)

    @pl.when(sec == 1)
    def _():
        pl.semaphore_wait(hello.at[0], 1)

    for c in range(2):
        far_first(c).start()
        near_first(c).start()
    to_rows(1)
    far_first(2).start()

    @pl.when((sec == 1) & (lo >= EARLY))
    def _():
        meet_far()

    @pl.loop(2, last)
    def _(g):
        to_rows(g)

    far_first(3).start()
    loads[1].wait()

    @pl.loop(0, ROWS // STEP)
    def _(g):
        own = own_mid[pl.ds(g * STEP + 1, STEP)].reshape(STEP * HALO, C)
        own = silu(jnp.dot(own, cp_ref[sec], preferred_element_type=jnp.float32))
        mid_out[pl.ds(g * STEP, STEP)] = own.astype(jnp.bfloat16).reshape(STEP, HALO, K)

    loads[2].wait()
    wet = wet_ref[...].astype(jnp.float32).astype(jnp.bfloat16)
    for dst, cols, first_col in ((wet_far, WIDE, HALO * odd), (wet_near, HALO, near_col)):
        slot = first_col + lax.broadcasted_iota(jnp.int32, (cols, COLS), 0)
        slot = (slot == lax.broadcasted_iota(jnp.int32, (cols, COLS), 1)).astype(jnp.bfloat16)
        dst[...] = jnp.dot(slot, wet, preferred_element_type=jnp.float32).astype(jnp.bfloat16)
    feat[...] = jnp.zeros_like(feat)

    @pl.loop(0, (ROWS + 2) * 2)
    def _(i):
        wide[pl.ds(i * EXT + 77, 5), :] = jnp.zeros((5, 128), jnp.float32)

    for copy in loads[3:]:
        copy.wait()

    def far_ready():
        @pl.when(sec == 0)
        def _():
            pl.semaphore_wait(hello.at[2], 1)

    def far_on(c):
        relay(far_first(c), far_second(c))

    def near_on(c):
        relay(near_first(c), near_second(c))

    @pl.when(sec == 1)
    def _():
        pl.semaphore_wait(hello.at[1], 1)

    near_on(0)
    near_on(1)

    @pl.when(lo >= EARLY)
    def _():
        far_ready()
        for c in range(3):
            far_on(c)

    features_hop(0).start()
    far_first(2).wait_send()
    far_first(4).start()

    @pl.when(lo >= EARLY)
    def _():
        far_on(3)

    features_hop(1).start()
    far_first(3).wait_send()
    far_first(5).start()

    @pl.when((sec == 1) & (lo < EARLY))
    def _():
        meet_far()

    @pl.when(lo < EARLY)
    def _():
        far_ready()
        for c in range(4):
            far_on(c)

    for side, row in enumerate((1, ROWS)):
        near_second(side).wait_recv()
        widen(halo_near, near_at, row, 1)
        far_second(side).wait_recv()
        widen(halo_far, far_at, row, 1)
        for half in range(2):
            lat_out[side, 0:EXT, halves[half]] = wide[pl.ds(at(row, half, 0), EXT), :].astype(jnp.bfloat16)
        lat_hop(side).start()

    @pl.loop(0, STEPS)
    def _(c):
        @pl.when(c == 0)
        def _():
            far_on(4)
            features_hop(2).start()
            far_first(4).wait_send()
            near_first(2).start()
            lat_hop(1).wait_recv()
            lat_row(1, la > 0)

        @pl.when(c == 1)
        def _():
            far_on(5)
            features_hop(3).start()
            far_first(5).wait_send()
            near_first(3).start()

        @pl.when(c == 2)
        def _():
            near_on(2)
            near_first(2).wait_send()
            near_first(4).start()

        @pl.when(c < STEPS - 1)
        def _():
            far_second(c + 2).wait_recv()
            widen(halo_far, far_at, STEP * c + 2, STEP)

        @pl.when(c == STEPS - 1)
        def _():
            near_on(3)
            near_first(3).wait_send()
            near_first(5).start()
            far_second(CHUNKS - 1).wait_recv()
            widen(halo_far, far_at, STEP * (STEPS - 1) + 2, STEP - 2)
            lat_hop(0).wait_recv()
            lat_row(0, la < n_lat - 1)

        features_hop(c).wait_recv()
        compute_far(c)

    @pl.loop(0, STEPS)
    def _(c):
        @pl.when(c == 0)
        def _():
            near_on(4)

        @pl.when(c == 1)
        def _():
            near_on(5)

        @pl.when(c < STEPS - 1)
        def _():
            near_second(c + 2).wait_recv()
            widen(halo_near, near_at, STEP * c + 2, STEP)

        @pl.when(c == STEPS - 1)
        def _():
            near_second(CHUNKS - 1).wait_recv()
            widen(halo_near, near_at, STEP * (STEPS - 1) + 2, STEP - 2)

        compute_near(c)

    for c in range(2):
        far_first(c).wait_send()
        near_first(c).wait_send()
    near_first(4).wait_send()
    near_first(5).wait_send()
    for c in range(CHUNKS):
        far_second(c).wait_send()
        near_second(c).wait_send()
    for c in range(STEPS):
        features_hop(c).wait_send()
    lat_hop(0).wait_send()
    lat_hop(1).wait_send()


def local(state, wet_mask, tap_offsets, conv_weight, couple_proj, couple_in, norm_gain, up_weight, down_weight):
    args = (
        state[0].transpose(1, 0, 2),
        wet_mask.T,
        tap_offsets.transpose(1, 2, 0),
        conv_weight[0].reshape(TAPS * C, C),
        couple_proj,
        couple_in[0],
        norm_gain,
        up_weight[0],
        down_weight[0],
    )
    dma = pltpu.SemaphoreType.DMA
    edge = pltpu.VMEM((ROWS + 2, HALO, C), jnp.bfloat16)
    out = pl.pallas_call(
        kernel,
        out_shape=jax.ShapeDtypeStruct((ROWS, COLS, C), jnp.bfloat16),
        in_specs=[pl.BlockSpec(memory_space=pltpu.HBM)] * len(args),
        out_specs=pl.BlockSpec(memory_space=pltpu.VMEM),
        scratch_shapes=[(pltpu.SMEM if i == 2 else pltpu.VMEM)(a.shape, a.dtype) for i, a in enumerate(args)]
        + [
            pltpu.VMEM(((ROWS + 2) * 2 * EXT, 128), jnp.float32),
        ]
        + [edge] * 7
        + [
            pltpu.VMEM((2, 96, C), jnp.bfloat16),
            pltpu.VMEM((2, 96, C), jnp.bfloat16),
            pltpu.VMEM((ROWS, HALO, K), jnp.bfloat16),
            pltpu.VMEM((ROWS, HALO, K), jnp.bfloat16),
            pltpu.VMEM((STEP, WIDE, K), jnp.float32),
            pltpu.VMEM((WIDE, ROWS), jnp.bfloat16),
            pltpu.VMEM((HALO, ROWS), jnp.bfloat16),
            pltpu.VMEM((STEP * WIDE, TAPS * C), jnp.bfloat16),
            dma((len(args),)),
            dma((4, CHUNKS)),
            dma((4, CHUNKS)),
            pltpu.SemaphoreType.REGULAR((3,)),
            dma((STEPS,)),
            dma((STEPS,)),
            dma((2,)),
            dma((2,)),
        ],
        compiler_params=pltpu.CompilerParams(
            collective_id=0, has_side_effects=True, vmem_limit_bytes=62 * 1024 * 1024
        ),
        cost_estimate=pl.CostEstimate(flops=6_000_000_000, bytes_accessed=5_000_000, transcendentals=2_000_000),
    )(*args)
    return out[None]


def solution(mesh):
    in_specs = (
        P("sec", "lat", "lon", None),
        P("lat", "lon"),
        P("lat", None, None),
        P("sec", None, None, None),
        P(),
        P("sec", None, None),
        P("sec", None),
        P("sec", None, None),
        P("sec", None, None),
    )
    out_specs = P("sec", "lat", "lon", None)
    return jax.shard_map(local, mesh=mesh, in_specs=in_specs, out_specs=out_specs, check_vma=False)
```

time: 55.5 us -> 53.4 us (0.962)
  the two profiles are of different devices: /device:TPU:24 before, /device:TPU:14 now
where the time goes in v3:
time: 53.4 us; the launch traced here: 53.2 us
  Pallas kernels  50.2 us (94%)
  local copies, waits for them, and re-layouts  3.02 us (6%)
    pallas_call x1, Pallas kernels, local(): pl.pallas_call(kernel, out_shape=jax.ShapeDtypeStruct((ROWS, COLS, C), jn...  50.2 us
    broadcast_in_dim x1, local copies, waits for them, and re-layouts, local(): return out[None]  3.02 us

profile of v3, /device:TPU:14, one launch (start us, length us, event | category | flops | bytes accessed | tf_op | source)
XLA Modules:
  0.0 53.2 jit_solution(13456159541110070648)
XLA Ops:
  0.0 50.2 %shard_map.91 = bf16[64,45,256]{2,1,0:T(8,128)(2,1)} custom-call(bf16[45,64,256]{2,1,0:T(8,128)(2,1)} %bitcast.11, s32[45,64]{1,0:T(8,128)} %bitcast.16, s32[3,3,64]{2,1,0:T(4,128)} %bitcast.17, bf16[2304,256]{1,0:T(8,128)(2,1)} %bitcast.12, bf16[2,256,128]{2,1,0:T(8,128)(2,1)} %cp_hbm.1, bf16[128,256]{1,0:T(8,128)(2,1)} %bitcast.15, f32[1,256]{1,0:T(1,128)} %gain_hbm.1, ...), custom_call_target="tpu_custom_call" | custom-call | flops 6000000000 | bytes 5000000 | tf_op jit(solution)/shard_map/pallas_call | solution.py:503
  50.2 3.0 %copy.10 = bf16[1,64,45,256]{3,1,2,0:T(8,128)(2,1)} copy(bf16[1,64,45,256]{3,2,1,0:T(8,128)(2,1)} %bitcast.10) | data formatting | bytes 2949120 | tf_op jit(solution)/shard_map/broadcast_in_dim | solution.py:536

commit v4 on v3

--- a/solution.py
+++ b/solution.py
@@ -17,6 +17,7 @@
 STEP = 16
 STEPS = ROWS // STEP
 CHUNKS = STEPS + 2
+MID = COLS - 2 * HALO
 WIDE = 32
 EARLY = 4
 LEAD = 4
@@ -35,7 +36,7 @@
     gain_hbm,
     up_hbm,
     down_hbm,
-    out_ref,
+    out_hbm,
     x_ref,
     wet_ref,
     off_ref,
@@ -47,7 +48,6 @@
     down_ref,
     wide,
     own_far,
-    own_mid,
     own_near,
     raw_far,
     raw_near,
@@ -61,7 +61,9 @@
     wet_far,
     wet_near,
     picks,
+    out_ref,
     load_sem,
+    store_sem,
     far_sem,
     near_sem,
     hello,
@@ -158,8 +160,8 @@
     def features_hop(c):
         rows = pl.ds(STEP * c, STEP)
         return pltpu.make_async_remote_copy(
-            src_ref=mid_out.at[rows],
-            dst_ref=mid_in.at[rows],
+            src_ref=mid_out.at[:, rows],
+            dst_ref=mid_in.at[:, rows],
             send_sem=f_send.at[c],
             recv_sem=f_recv.at[c],
             device_id=partner,
@@ -176,6 +178,10 @@
             device_id_type=MESH,
         )
 
+    def store(c):
+        rows = pl.ds(STEP * c, STEP)
+        return pltpu.make_async_copy(out_ref.at[rows], out_hbm.at[rows], store_sem.at[c])
+
     def silu(v):
         return v * (0.5 + 0.5 * jnp.tanh(0.5 * v))
 
@@ -199,7 +205,7 @@
         def _(i):
             row = base + 1 + i
             for half in range(2):
-                for dst, col in ((own_far, far_col), (own_mid, 16), (own_near, near_col)):
+                for dst, col in ((own_far, far_col), (own_near, near_col)):
                     dst[row, :, halves[half]] = wide[pl.ds(at(row, half, HALO + col), HALO), :].astype(jnp.bfloat16)
 
     def widen(halo, where, start, rows):
@@ -265,19 +271,12 @@
     def compute_far(c):
         base = c * STEP
         rows = pl.ds(base, STEP)
-        edge = edge_features(raw_far, base).reshape(STEP, HALO, K)
-        mid = mid_in[rows].astype(jnp.float32)
-        feat[:, 0:16] = jnp.where(odd == 0, edge, mid)
-
-        @pl.when(odd == 0)
-        def _():
-            feat[:, 16:32] = mid
-
-        @pl.when(odd == 1)
-        def _():
-            feat[:, 13:29] = edge
-
-        result = compute(base, WIDE, HALO * odd, feat[...].reshape(STEP * WIDE, K), wet_far)
+        edge = edge_features(raw_far, base)
+        for i in range(STEP):
+            feat[pl.ds(i * WIDE + MID * odd, HALO), :] = edge[i * HALO : (i + 1) * HALO]
+        for col in range(MID):
+            feat[pl.ds(HALO * (1 - odd) + col, STEP, WIDE), :] = mid_in[col, rows].astype(jnp.float32)
+        result = compute(base, WIDE, HALO * odd, feat[...], wet_far)
 
         @pl.when(odd == 0)
         def _():
@@ -332,11 +331,10 @@
     far_first(3).start()
     loads[1].wait()
 
-    @pl.loop(0, ROWS // STEP)
-    def _(g):
-        own = own_mid[pl.ds(g * STEP + 1, STEP)].reshape(STEP * HALO, C)
-        own = silu(jnp.dot(own, cp_ref[sec], preferred_element_type=jnp.float32))
-        mid_out[pl.ds(g * STEP, STEP)] = own.astype(jnp.bfloat16).reshape(STEP, HALO, K)
+    @pl.loop(0, MID)
+    def _(col):
+        own = jnp.dot(x_ref[HALO + col], cp_ref[sec], preferred_element_type=jnp.float32)
+        mid_out[col] = silu(own).astype(jnp.bfloat16)
 
     loads[2].wait()
     wet = wet_ref[...].astype(jnp.float32).astype(jnp.bfloat16)
@@ -377,7 +375,6 @@
         for c in range(3):
             far_on(c)
 
-    features_hop(0).start()
     far_first(2).wait_send()
     far_first(4).start()
 
@@ -385,7 +382,6 @@
     def _():
         far_on(3)
 
-    features_hop(1).start()
     far_first(3).wait_send()
     far_first(5).start()
 
@@ -398,6 +394,16 @@
         far_ready()
         for c in range(4):
             far_on(c)
+
+    far_on(4)
+    far_first(4).wait_send()
+    features_hop(0).start()
+    features_hop(1).start()
+
+    far_on(5)
+    far_first(5).wait_send()
+    features_hop(2).start()
+    features_hop(3).start()
 
     for side, row in enumerate((1, ROWS)):
         near_second(side).wait_recv()
@@ -412,18 +418,12 @@
     def _(c):
         @pl.when(c == 0)
         def _():
-            far_on(4)
-            features_hop(2).start()
-            far_first(4).wait_send()
             near_first(2).start()
             lat_hop(1).wait_recv()
             lat_row(1, la > 0)
 
         @pl.when(c == 1)
         def _():
-            far_on(5)
-            features_hop(3).start()
-            far_first(5).wait_send()
             near_first(3).start()
 
         @pl.when(c == 2)
@@ -471,6 +471,7 @@
             widen(halo_near, near_at, STEP * (STEPS - 1) + 2, STEP - 2)
 
         compute_near(c)
+        store(c).start()
 
     for c in range(2):
         far_first(c).wait_send()
@@ -484,6 +485,8 @@
         features_hop(c).wait_send()
     lat_hop(0).wait_send()
     lat_hop(1).wait_send()
+    for c in range(STEPS):
+        store(c).wait()
 
 
 def local(state, wet_mask, tap_offsets, conv_weight, couple_proj, couple_in, norm_gain, up_weight, down_weight):
@@ -504,22 +507,24 @@
         kernel,
         out_shape=jax.ShapeDtypeStruct((ROWS, COLS, C), jnp.bfloat16),
         in_specs=[pl.BlockSpec(memory_space=pltpu.HBM)] * len(args),
-        out_specs=pl.BlockSpec(memory_space=pltpu.VMEM),
+        out_specs=pl.BlockSpec(memory_space=pl.ANY),
         scratch_shapes=[(pltpu.SMEM if i == 2 else pltpu.VMEM)(a.shape, a.dtype) for i, a in enumerate(args)]
         + [
             pltpu.VMEM(((ROWS + 2) * 2 * EXT, 128), jnp.float32),
         ]
-        + [edge] * 7
+        + [edge] * 6
         + [
             pltpu.VMEM((2, 96, C), jnp.bfloat16),
             pltpu.VMEM((2, 96, C), jnp.bfloat16),
-            pltpu.VMEM((ROWS, HALO, K), jnp.bfloat16),
-            pltpu.VMEM((ROWS, HALO, K), jnp.bfloat16),
-            pltpu.VMEM((STEP, WIDE, K), jnp.float32),
+            pltpu.VMEM((MID, ROWS, K), jnp.bfloat16),
+            pltpu.VMEM((MID, ROWS, K), jnp.bfloat16),
+            pltpu.VMEM((STEP * WIDE, K), jnp.float32),
             pltpu.VMEM((WIDE, ROWS), jnp.bfloat16),
             pltpu.VMEM((HALO, ROWS), jnp.bfloat16),
             pltpu.VMEM((STEP * WIDE, TAPS * C), jnp.bfloat16),
+            pltpu.VMEM((ROWS, COLS, C), jnp.bfloat16),
             dma((len(args),)),
+            dma((STEPS,)),
             dma((4, CHUNKS)),
             dma((4, CHUNKS)),
             pltpu.SemaphoreType.REGULAR((3,)),

time: 53.4 us -> 49 us (0.918)
  the two profiles are of different devices: /device:TPU:14 before, /device:TPU:24 now
where the time goes in v4:
time: 49 us; the launch traced here: 48.3 us
  Pallas kernels  45.2 us (92%)
  local copies, waits for them, and re-layouts  3.02 us (6%)
    pallas_call x1, Pallas kernels, local(): pl.pallas_call(kernel, out_shape=jax.ShapeDtypeStruct((ROWS, COLS, C), jn...  45.2 us
    broadcast_in_dim x1, local copies, waits for them, and re-layouts, local(): return out[None]  3.02 us

profile of v4, /device:TPU:24, one launch (start us, length us, event | category | flops | bytes accessed | tf_op | source)
XLA Modules:
  0.0 48.3 jit_solution(14665915131718036484)
XLA Ops:
  0.0 45.2 %shard_map.91 = bf16[64,45,256]{2,1,0:T(8,128)(2,1)} custom-call(bf16[45,64,256]{2,1,0:T(8,128)(2,1)} %bitcast.11, s32[45,64]{1,0:T(8,128)} %bitcast.16, s32[3,3,64]{2,1,0:T(4,128)} %bitcast.17, bf16[2304,256]{1,0:T(8,128)(2,1)} %bitcast.12, bf16[2,256,128]{2,1,0:T(8,128)(2,1)} %cp_hbm.1, bf16[128,256]{1,0:T(8,128)(2,1)} %bitcast.15, f32[1,256]{1,0:T(1,128)} %gain_hbm.1, ...), custom_call_target="tpu_custom_call" | custom-call | flops 6000000000 | bytes 5000000 | tf_op jit(solution)/shard_map/pallas_call | solution.py:506
  45.3 3.0 %copy.10 = bf16[1,64,45,256]{3,1,2,0:T(8,128)(2,1)} copy(bf16[1,64,45,256]{3,2,1,0:T(8,128)(2,1)} %bitcast.10) | data formatting | bytes 2949120 | tf_op jit(solution)/shard_map/broadcast_in_dim | solution.py:541

commit v5 on v4

--- a/solution.py
+++ b/solution.py
@@ -304,6 +304,10 @@
     to_rows(0)
     to_rows(last)
 
+    @pl.when((sec == 1) & (lo >= EARLY))
+    def _():
+        meet_far()
+
     @pl.when(sec == 0)
     def _():
         pl.semaphore_wait(barrier, 4)
@@ -319,10 +323,6 @@
         near_first(c).start()
     to_rows(1)
     far_first(2).start()
-
-    @pl.when((sec == 1) & (lo >= EARLY))
-    def _():
-        meet_far()
 
     @pl.loop(2, last)
     def _(g):

time: 49 us -> 49 us (level)
  no operation moved by 1% of the time
where the time goes in v5:
time: 49 us; the launch traced here: 48.3 us
  Pallas kernels  45.3 us (92%)
  local copies, waits for them, and re-layouts  3.02 us (6%)
    pallas_call x1, Pallas kernels, local(): pl.pallas_call(kernel, out_shape=jax.ShapeDtypeStruct((ROWS, COLS, C), jn...  45.3 us
    broadcast_in_dim x1, local copies, waits for them, and re-layouts, local(): return out[None]  3.02 us

profile of v5, /device:TPU:24, one launch (start us, length us, event | category | flops | bytes accessed | tf_op | source)
XLA Modules:
  0.0 48.3 jit_solution(10889035328858868182)
XLA Ops:
  0.0 45.3 %shard_map.91 = bf16[64,45,256]{2,1,0:T(8,128)(2,1)} custom-call(bf16[45,64,256]{2,1,0:T(8,128)(2,1)} %bitcast.11, s32[45,64]{1,0:T(8,128)} %bitcast.16, s32[3,3,64]{2,1,0:T(4,128)} %bitcast.17, bf16[2304,256]{1,0:T(8,128)(2,1)} %bitcast.12, bf16[2,256,128]{2,1,0:T(8,128)(2,1)} %cp_hbm.1, bf16[128,256]{1,0:T(8,128)(2,1)} %bitcast.15, f32[1,256]{1,0:T(1,128)} %gain_hbm.1, ...), custom_call_target="tpu_custom_call" | custom-call | flops 6000000000 | bytes 5000000 | tf_op jit(solution)/shard_map/pallas_call | solution.py:506
  45.3 3.0 %copy.10 = bf16[1,64,45,256]{3,1,2,0:T(8,128)(2,1)} copy(bf16[1,64,45,256]{3,2,1,0:T(8,128)(2,1)} %bitcast.10) | data formatting | bytes 2949120 | tf_op jit(solution)/shard_map/broadcast_in_dim | solution.py:541
